TPU v7x, 32 devices: a whole 2x2x4 slice. The times are simulated.
32 devices in a mesh: dom: 8 (over y, x, core), case: 4 (over z).
Axes of the slice: x: 2, y: 2, z: 4, core: 2. Of those that a mesh axis runs over, the one named last changes fastest.
Arguments:
- displacement: float32 [64, 6, 32768], P('case', None, 'dom'), may hold values from -6 to 6
- adjoint: float32 [64, 6, 32768], P('case', None, 'dom'), may hold values from -6 to 6
- stiffness_ref: float32 [24, 24], replicated, may hold values from -0.25 to 0.25
- element_scale: float32 [8192], P('dom'), may hold values from 0.5 to 4
- connectivity: int32 [4, 8192], P(None, 'dom'), may hold values from 0 to 5119
- shared_nodes: int32 [2, 4096], P(None, 'dom'), may hold values from 0 to 4095
- spline_node: int32 [64, 128], P('dom'), may hold values from 0 to 4095
- spline_panel: int32 [64, 128], P('dom'), may hold values from 0 to 63
- spline_weight: float32 [64, 128], P('dom'), may hold values from -2 to 2
- spline_count: int32 [64], P('dom'), may hold values from 1 to 128, as said below
- case_weight: float32 [64], P('case'), may hold values from 0.3 to 3
Outputs:
- thickness_grad: float32 [8192], P(('dom', 'case'))
- panel_grad: float32 [512], P(('dom', 'case'))
Inputs may be any that keep to these rules, and one draw needn't show every extreme that they name: `spline_count`: in each partition's 8 entries some entry equals 128.
All inputs are finite; a program needn't handle non-finite values.
Results may differ from a plain program's by a relative error of at most 0.0003.
Values sent between devices are 32-bit elements; how exact they have to be, the bound alone decides.
A program may use at most 128 MiB of HBM per device.

v0:
```python
import math

import jax
import jax.numpy as jnp
from jax import lax
from jax.sharding import PartitionSpec as P

PANELS_DEV = 64


def passed_along(value, axis, steps):
    count = lax.axis_size(axis)
    initial, last = (max(0, -steps), min(count, count - steps))
    return lax.ppermute(value, axis, [(source, source + steps) for source in range(initial, last)])


def on_device(
    displacement,
    adjoint,
    stiffness_ref,
    element_scale,
    connectivity,
    shared_nodes,
    spline_node,
    spline_panel,
    spline_weight,
    spline_count,
    case_weight,
):
    local_cases = displacement.shape[0]
    block_size = local_cases // 2
    groups = lax.axis_size("case")
    components = displacement.shape[1]
    corner_count = connectivity.shape[0]
    elements = connectivity.shape[1]
    node_major = jnp.stack(
        [jnp.transpose(displacement, (2, 0, 1)), jnp.transpose(adjoint, (2, 0, 1))], axis=1
    )
    to_lower = node_major[shared_nodes[0]]
    to_upper = node_major[shared_nodes[1]]
    from_upper = passed_along(to_lower, "dom", -1)
    from_lower = passed_along(to_upper, "dom", 1)
    slot_ids = lax.broadcasted_iota(jnp.int32, spline_weight.shape, 1)
    coefficient = jnp.where(slot_ids < spline_count[:, None], spline_weight, 0.0)
    vertical = jnp.concatenate([displacement[:, 2, :], adjoint[:, 2, :]], axis=0)
    values = vertical[:, spline_node] * coefficient[None]
    panel_ids = lax.broadcasted_iota(jnp.int32, (1, 1, PANELS_DEV), 2)
    received, targets = (
        lax.all_to_all(values, "dom", split_axis=1, concat_axis=1, tiled=True),
        lax.all_to_all(spline_panel[None], "dom", split_axis=1, concat_axis=1, tiled=True),
    )
    onehot = (targets[0][:, :, None] == panel_ids).astype(jnp.float32)
    washes = jnp.einsum("ksq,sqp->kp", received, onehot, precision=lax.Precision.HIGHEST)
    product = washes[:local_cases] * washes[local_cases:]
    extended = jnp.concatenate([node_major, from_lower, from_upper], axis=0)
    flat_rows = extended.reshape(extended.shape[0], 2 * local_cases * components)
    gathered = flat_rows[connectivity.reshape(-1)].reshape(
        corner_count, elements, 2, local_cases, components
    )
    reshaped_ref = stiffness_ref.reshape(components, corner_count, components, corner_count)
    stiffness = jnp.einsum(
        "ikjl,lecj->keci", reshaped_ref, gathered[:, :, 0], precision=lax.Precision.HIGHEST
    )
    energy = jnp.einsum(
        "keci,keci->ce", gathered[:, :, 1], stiffness, precision=lax.Precision.HIGHEST
    )
    thick_sum = 0.0
    panel_sum = 0.0
    for offset in (0, block_size):
        weights = case_weight[offset : offset + block_size]
        thick_part = jnp.dot(
            weights, energy[offset : offset + block_size], precision=lax.Precision.HIGHEST
        )
        panel_part = jnp.dot(
            weights, product[offset : offset + block_size], precision=lax.Precision.HIGHEST
        )
        reduced = (
            lax.psum_scatter(thick_part, "case", scatter_dimension=0, tiled=True),
            lax.psum_scatter(panel_part, "case", scatter_dimension=0, tiled=True),
        )
        thick_sum = thick_sum + reduced[0]
        panel_sum = panel_sum + reduced[1]
    position = lax.axis_index("case")
    share_size = element_scale.shape[0] // groups
    scaling = lax.dynamic_slice_in_dim(element_scale, position * share_size, share_size, 0)
    factor_root = math.sqrt(local_cases * groups)
    return (-scaling * thick_sum / factor_root, panel_sum / factor_root)


def solution(mesh):
    return jax.shard_map(
        on_device,
        mesh=mesh,
        in_specs=(
            P("case", None, "dom"),
            P("case", None, "dom"),
            P(),
            P("dom"),
            P(None, "dom"),
            P(None, "dom"),
            P("dom", None),
            P("dom", None),
            P("dom", None),
            P("dom"),
            P("case"),
        ),
        out_specs=(P(("dom", "case")), P(("dom", "case"))),
        check_vma=False,
    )
```

profile of v0, /device:TPU:0, one launch (start us, length us, event | category | flops | bytes accessed | tf_op | source)
XLA Modules:
  0.0 158.2 jit_solution(16167548711277374955)
XLA Ops:
  0.6 2.1 %pad_maximum_fusion.1 = f32[4096,2,16,6]{0,2,3,1:T(8,128)S(1)} fusion(f32[4096,1,16,6]{0,2,3,1:T(8,128)} %bitcast.80, f32[4096,1,16,6]{0,2,3,1:T(8,128)} %bitcast.82), kind=kLoop, calls=%fused_computation.5 | loop fusion | flops 786432 | bytes 6291456 | tf_op jit(solution)/shard_map/stack | solution.py:36
  2.7 0.0 copy-start.6
  2.7 24.6 %copy.35 = f32[4096,2,16,6]{2,1,3,0:T(2,128)} copy(f32[4096,2,16,6]{0,2,3,1:T(8,128)S(1)} %pad_maximum_fusion.1) | data formatting | bytes 6291456 | tf_op jit(solution)/shard_map/stack | solution.py:36
  27.3 0.0 copy-done.6
  27.3 12.4 %gather_fusion = f32[512,2,16,6]{2,1,3,0:T(2,128)S(1)} fusion(f32[4096,2,16,6]{2,1,3,0:T(2,128)} %copy.35, s32[1024]{0:T(1024)S(1)} %pad_clamp_fusion.1), kind=kCustom, calls=%fused_computation | custom fusion | bytes 788480 | tf_op jit(solution)/shard_map/gather | solution.py:40
  39.7 3.3 %copy.36 = f32[512,2,16,6]{0,2,3,1:T(8,128)} copy(f32[512,2,16,6]{2,1,3,0:T(2,128)S(1)} %gather_fusion) | data formatting | bytes 786432 | tf_op jit(solution)/shard_map/gather | solution.py:40
  43.1 3.1 %collective-permute-start = (f32[512,2,16,6]{0,2,3,1:T(8,128)}, f32[512,2,16,6]{0,2,3,1:T(8,128)}, u32[]{:S(2)}, u32[]{:S(2)}) collective-permute-start(f32[512,2,16,6]{0,2,3,1:T(8,128)} %copy.36), channel_id=1, source_target_pairs={{0,4},{4,8},{8,12},{12,16},{16,20},{20,24},{24,28},{1,5},{5,9},{9,... | collective-permute-start | bytes 1179656 | tf_op jit(solution)/shard_map/ppermute | solution.py:14
  46.2 12.4 %gather_fusion.1 = f32[512,2,16,6]{2,1,3,0:T(2,128)S(1)} fusion(f32[4096,2,16,6]{2,1,3,0:T(2,128)} %copy.35, s32[1024]{0:T(1024)S(1)} %pad_clamp_fusion), kind=kCustom, calls=%fused_computation.1 | custom fusion | bytes 788480 | tf_op jit(solution)/shard_map/gather | solution.py:39
  58.6 0.0 copy-start.3
  58.6 3.3 %copy.38 = f32[512,2,16,6]{0,2,3,1:T(8,128)} copy(f32[512,2,16,6]{2,1,3,0:T(2,128)S(1)} %gather_fusion.1) | data formatting | bytes 786432 | tf_op jit(solution)/shard_map/gather | solution.py:39
  61.9 0.0 copy-start.7
  61.9 1.4 collective-permute-start.1
  63.4 6.3 %all-to-all-start.1 = ((s32[1,8,128]{2,0,1:T(1,128)}), s32[1,8,128]{2,0,1:T(1,128)S(1)}, u32[]{:S(2)}, u32[]{:S(2)}) async-start(s32[1,8,128]{2,0,1:T(1,128)} %bitcast.31), calls=%async_computation.1 | async-start | bytes 8192 | tf_op jit(solution)/shard_map/all_to_all | solution.py:50
  69.7 0.0 copy-start.8
  69.7 0.0 copy-start.9
  69.7 1.1 slice_bitcast_fusion.3
  70.8 0.0 copy-start.4
  70.8 0.0 copy-start.10
  70.8 0.0 copy-done.3
  70.9 0.0 copy-start.5
  70.9 0.0 copy-start.1
  70.9 0.0 copy-start.2
  70.9 0.8 pad_maximum_fusion.2
  71.8 3.3 %copy.43 = f32[32,4096]{0,1:T(8,128)} copy(f32[32,4096]{1,0:T(8,128)} %pad_maximum_fusion.2) | data formatting | bytes 1048576 | tf_op jit(solution)/shard_map/concatenate | solution.py:45
  75.0 0.0 copy-done.7
  75.0 5.6 %gather_fusion.3 = f32[1024,32]{1,0:T(8,128)} fusion(f32[32,4096]{0,1:T(8,128)} %copy.43, s32[1024]{0:T(1024)S(1)} %fusion.9), kind=kCustom, calls=%fused_computation.3 | custom fusion | bytes 266240 | tf_op jit(solution)/shard_map/gather | solution.py:46
  80.7 1.2 copy.45
  81.9 0.0 copy-done.8
  81.9 0.0 copy-done.9
  81.9 0.1 fusion.12
  82.0 0.7 multiply_bitcast_fusion
  82.6 0.0 copy-done.4
  82.6 0.1 reshape.106
  82.7 0.3 copy.42
  83.0 0.0 copy-done.10
  83.0 0.6 dynamic-slice
  84.9 0.0 all-to-all-done.1
  84.9 4.2 %all-to-all-start = ((f32[32,8,128]{2,0,1:T(8,128)}), f32[32,8,128]{2,0,1:T(8,128)S(1)}, u32[]{:S(2)}, u32[]{:S(2)}) async-start(f32[32,8,128]{2,0,1:T(8,128)} %multiply_bitcast_fusion), calls=%async_computation | async-start | bytes 262144 | tf_op jit(solution)/shard_map/all_to_all | solution.py:49
  89.1 5.5 %all-to-all-done = f32[32,8,128]{2,0,1:T(8,128)S(1)} async-done(((f32[32,8,128]{2,0,1:T(8,128)}), f32[32,8,128]{2,0,1:T(8,128)S(1)}, u32[]{:S(2)}, u32[]{:S(2)}) %all-to-all-start) | async-done | bytes 131104 | tf_op jit(solution)/shard_map/all_to_all | solution.py:49
  94.6 0.2 convolution_bitcast_fusion
  94.9 0.0 copy-done.5
  94.9 0.2 convolution_bitcast_fusion.1
  95.1 0.1 fusion.1
  95.2 0.0 collective-permute-done
  95.2 0.0 collective-permute-done.1
  95.2 0.0 copy-done.1
  95.3 0.0 copy-done.2
  95.3 1.4 pad_maximum_fusion
  96.6 4.7 %copy.39 = f32[5120,2,16,6]{0,3,2,1:T(8,128)} copy(f32[5120,2,16,6]{0,2,3,1:T(8,128)S(1)} %pad_maximum_fusion) | data formatting | bytes 7864320 | tf_op jit(solution)/shard_map/concatenate | solution.py:55
  101.3 5.1 %reshape.103 = f32[5120,192]{0,1:T(8,128)} reshape(f32[5120,2,16,6]{0,3,2,1:T(8,128)} %copy.39) | data formatting | bytes 7864320 | tf_op jit(solution)/shard_map/reshape | solution.py:56
  106.4 5.6 %copy.40 = f32[5120,192]{1,0:T(8,128)} copy(f32[5120,192]{0,1:T(8,128)} %reshape.103) | data formatting | bytes 7864320 | tf_op jit(solution)/shard_map/reshape | solution.py:56
  112.0 18.7 %gather_fusion.2 = f32[4096,192]{1,0:T(8,128)} fusion(f32[5120,192]{1,0:T(8,128)} %copy.40, s32[4096]{0:T(1024)S(1)} %broadcast_clamp_fusion), kind=kCustom, calls=%fused_computation.2 | custom fusion | bytes 6307840 | tf_op jit(solution)/shard_map/gather | solution.py:57
  130.7 3.7 %copy.41 = f32[4096,192]{0,1:T(8,128)S(1)} copy(f32[4096,192]{1,0:T(8,128)} %gather_fusion.2) | data formatting | bytes 6291456 | tf_op jit(solution)/shard_map/gather | solution.py:57
  134.4 3.4 %reshape.105 = f32[4,1024,2,16,6]{1,0,4,3,2:T(4,128)} reshape(f32[4096,192]{0,1:T(8,128)S(1)} %copy.41) | data formatting | bytes 6291456 | tf_op jit(solution)/shard_map/reshape | solution.py:57
  137.8 0.0 copy-start
  137.8 1.7 %slice_bitcast_fusion.2 = f32[16,1024,6,4]{1,3,2,0:T(4,128)S(1)} fusion(f32[4,1024,2,16,6]{1,0,4,3,2:T(4,128)} %reshape.105), kind=kLoop, calls=%fused_computation.9 | loop fusion | bytes 3145728
  139.6 0.6 copy-done
  140.2 3.5 %fusion = f32[16,1024]{1,0:T(8,128)S(1)} fusion(f32[16,1024,6,4]{1,3,2,0:T(4,128)S(1)} %slice_bitcast_fusion.2, f32[4,1024,2,16,6]{1,0,4,3,2:T(4,128)S(1)} %copy-done, f32[6,4,6,4]{0,3,2,1:T(4,128)S(1)} %copy.42), kind=kOutput, calls=%fused_computation.7 | convolution fusion | flops 114016256 | bytes 3260416 | tf_op jit(solution)/shard_map/ikjl,lecj->keci/dot_general | solution.py:61
  143.7 0.2 fusion.6
  143.9 0.2 fusion.4
  144.1 12.1 %all-reduce.2 = (f32[1024]{0:T(1024)S(1)}, f32[64]{0:T(128)S(1)}) all-reduce(f32[1024]{0:T(1024)S(1)} %add.65, f32[64]{0:T(128)S(1)} %fusion.1), channel_id=4, replica_groups=mesh['dom'=8,'case'=4] {'case'}, use_global_device_ids=true, to_apply=%region_0.1.clone | all-reduce | flops 1088 | bytes 8704
  156.2 0.6 dynamic-slice_multiply_fusion.1
  156.8 1.3 fusion.13
  (9 shorter events, 0.1 us)
Async XLA Ops:
  2.7 24.6 %copy-start.6 = (s32[2,512]{1,0:T(2,128)S(1)}, s32[2,512]{1,0:T(2,128)}, u32[]{:S(2)}) copy-start(s32[2,512]{1,0:T(2,128)} %param.16) | copy-start | bytes 12292
  43.1 52.2 %collective-permute-start = (f32[512,2,16,6]{0,2,3,1:T(8,128)}, f32[512,2,16,6]{0,2,3,1:T(8,128)}, u32[]{:S(2)}, u32[]{:S(2)}) collective-permute-start(f32[512,2,16,6]{0,2,3,1:T(8,128)} %copy.36), channel_id=1, source_target_pairs={{0,4},{4,8},{8,12},{12,16},{16,20},{20,24},{24,28},{1,5},{5,9},{9,... | collective-permute-start | bytes 1179656 | tf_op jit(solution)/shard_map/ppermute | solution.py:14
  58.6 12.2 %copy-start.3 = (s32[4,1024]{1,0:T(4,128)S(1)}, s32[4,1024]{1,0:T(4,128)}, u32[]{:S(2)}) copy-start(s32[4,1024]{1,0:T(4,128)} %param.15) | copy-start | bytes 49156
  61.9 13.1 %copy-start.7 = (s32[8,128]{1,0:T(8,128)S(1)}, s32[8,128]{1,0:T(8,128)}, u32[]{:S(2)}) copy-start(s32[8,128]{1,0:T(8,128)} %param.17) | copy-start | bytes 12292
  61.9 33.3 %collective-permute-start.1 = (f32[512,2,16,6]{0,2,3,1:T(8,128)}, f32[512,2,16,6]{0,2,3,1:T(8,128)}, u32[]{:S(2)}, u32[]{:S(2)}) collective-permute-start(f32[512,2,16,6]{0,2,3,1:T(8,128)} %copy.38), channel_id=1, source_target_pairs={{4,0},{8,4},{12,8},{16,12},{20,16},{24,20},{28,24},{5,1},{9,5},{13... | collective-permute-start | bytes 1179656 | tf_op jit(solution)/shard_map/ppermute | solution.py:14
  63.4 21.5 %all-to-all-start.1 = ((s32[1,8,128]{2,0,1:T(1,128)}), s32[1,8,128]{2,0,1:T(1,128)S(1)}, u32[]{:S(2)}, u32[]{:S(2)}) async-start(s32[1,8,128]{2,0,1:T(1,128)} %bitcast.31), calls=%async_computation.1 | async-start | bytes 8192 | tf_op jit(solution)/shard_map/all_to_all | solution.py:50
  69.7 12.2 %copy-start.8 = (f32[8,128]{1,0:T(8,128)S(1)}, f32[8,128]{1,0:T(8,128)}, u32[]{:S(2)}) copy-start(f32[8,128]{1,0:T(8,128)} %param.19) | copy-start | bytes 12292
  69.7 12.2 %copy-start.9 = (s32[8]{0:T(128)S(1)}, s32[8]{0:T(128)}, u32[]{:S(2)}) copy-start(s32[8]{0:T(128)} %param.20) | copy-start | bytes 100
  70.8 11.8 %copy-start.4 = (f32[24,24]{1,0:T(8,128)S(1)}, f32[24,24]{1,0:T(8,128)}, u32[]{:S(2)}) copy-start(f32[24,24]{1,0:T(8,128)} %param.13) | copy-start | bytes 6916
  70.8 12.2 %copy-start.10 = (u32[32]{0:T(128)S(1)}, u32[32]{0:T(128)}, u32[]{:S(2)}) copy-start(u32[32]{0:T(128)} %constant.28) | copy-start | bytes 388
  70.9 24.0 %copy-start.5 = (f32[16]{0:T(128)S(1)}, f32[16]{0:T(128)}, u32[]{:S(2)}) copy-start(f32[16]{0:T(128)} %param.21) | copy-start | bytes 196
  70.9 24.3 %copy-start.1 = (f32[16,6,4096]{2,0,1:T(8,128)S(1)}, f32[16,6,4096]{2,0,1:T(8,128)}, u32[]{:S(2)}) copy-start(f32[16,6,4096]{2,0,1:T(8,128)} %param.12) | copy-start | bytes 4718596
  70.9 24.3 %copy-start.2 = (f32[16,6,4096]{2,0,1:T(8,128)S(1)}, f32[16,6,4096]{2,0,1:T(8,128)}, u32[]{:S(2)}) copy-start(f32[16,6,4096]{2,0,1:T(8,128)} %param.11) | copy-start | bytes 4718596
  84.9 9.7 %all-to-all-start = ((f32[32,8,128]{2,0,1:T(8,128)}), f32[32,8,128]{2,0,1:T(8,128)S(1)}, u32[]{:S(2)}, u32[]{:S(2)}) async-start(f32[32,8,128]{2,0,1:T(8,128)} %multiply_bitcast_fusion), calls=%async_computation | async-start | bytes 262144 | tf_op jit(solution)/shard_map/all_to_all | solution.py:49
  137.8 2.4 %copy-start = (f32[4,1024,2,16,6]{1,0,4,3,2:T(4,128)S(1)}, f32[4,1024,2,16,6]{1,0,4,3,2:T(4,128)}, u32[]{:S(2)}) copy-start(f32[4,1024,2,16,6]{1,0,4,3,2:T(4,128)} %reshape.105) | copy-start | bytes 9437188
where the time goes:
time: 159 us; the launch traced here: 158 us
  local copies, waits for them, and re-layouts  112 us (70%)
  starting transfers between devices  15.1 us (9%)
  blocking collectives  12.1 us (8%)
  other arithmetic  7 us (4%)
  waiting for transfers between devices  5.54 us (3%)
  matrix products  4.43 us (3%)
  between operations  2.24 us (1%)
    another operation x1, local copies, waits for them, and re-layouts, on_device(): jnp.stack([jnp.transpose(displacement, (2, 0, 1)), jnp.transpose(adjoint,...  24.6 us
    gather x2, local copies, waits for them, and re-layouts, on_device(): flat_rows[connectivity.reshape(-1)]  22.4 us
    gather x2, local copies, waits for them, and re-layouts, on_device(): to_upper = node_major[shared_nodes[1]]  15.7 us
    gather x2, local copies, waits for them, and re-layouts, on_device(): to_lower = node_major[shared_nodes[0]]  15.7 us
    unnamed x1, blocking collectives  12.1 us
    reshape x2, local copies, waits for them, and re-layouts, on_device(): extended.reshape(extended.shape[0], 2 * local_cases * components)  10.7 us
    gather x2, local copies, waits for them, and re-layouts, on_device(): values = vertical[:, spline_node] * coefficient[None]  6.84 us
    all_to_all x1, starting transfers between devices, on_device(): lax.all_to_all(spline_panel[None], 'dom', split_axis=1, concat_axis=1, ti...  6.34 us
  transfers between devices with their start and end apart: 4, of which 1 were waited for; matrix products, arithmetic and copies ran while one was open for 19% of the time, Pallas kernels for 0%

commit v1 on v0

v1 whole, which is shorter than its diff:
```python
import functools
import math

import jax
import jax.numpy as jnp
from jax import lax
from jax.experimental import pallas as pl
from jax.experimental.pallas import tpu as pltpu
from jax.sharding import PartitionSpec as P

PANELS_DEV = 64
LANES = 128
HIGHEST = lax.Precision.HIGHEST
MESH = pl.DeviceIdType.MESH
PACK = (0, 16, 64, 80)


def iota(shape, dim):
    return lax.broadcasted_iota(jnp.int32, shape, dim)


def dot_lanes(a, b):
    return lax.dot_general(
        a, b, (((1,), (1,)), ((), ())), precision=HIGHEST, preferred_element_type=jnp.float32
    )


def kernel(
    n_dom,
    groups,
    u_ref,
    a_ref,
    k_ref,
    scale_ref,
    panel_ref,
    weight_ref,
    conn_ref,
    shared_ref,
    node_ref,
    count_ref,
    case_ref,
    thick_ref,
    wash_ref,
    table,
    picked,
    halo_pick,
    halo_out,
    halo_in,
    spline_pick,
    spline_out,
    spline_in,
    big_hi,
    big_lo,
    thick,
    message,
    arrived,
    halo_send,
    halo_recv,
    spline_send,
    spline_recv,
    case_send,
    case_recv,
):
    cases = case_ref.shape[0]
    nodes = u_ref.shape[1]
    corners, elements = conn_ref.shape
    shared = shared_ref.shape[1]
    slots = node_ref.shape[1]
    half = shared // 2
    share_rows = elements // LANES // groups
    dom, case = lax.axis_index("dom"), lax.axis_index("case")

    barrier = pltpu.get_barrier_semaphore()
    for off in range(1, n_dom):
        pl.semaphore_signal(
            barrier, inc=1, device_id=(lax.rem(dom + off, n_dom), case), device_id_type=MESH
        )
    for off in range(1, groups):
        pl.semaphore_signal(
            barrier, inc=1, device_id=(dom, lax.rem(case + off, groups)), device_id_type=MESH
        )

    rest = u_ref.shape[0] - 32

    def turn(block, carry):
        cols = pl.ds(pl.multiple_of(block * LANES, LANES), LANES)
        first = jnp.concatenate([u_ref[:, cols], a_ref[0:32, cols]], axis=0)
        second = jnp.concatenate(
            [a_ref[32 : 32 + rest, cols], jnp.zeros((LANES - rest, LANES), jnp.float32)], axis=0
        )
        start = pl.multiple_of(block * 2 * LANES, 2 * LANES)
        table[pl.ds(start, LANES, stride=2), :] = first.T
        table[pl.ds(start + 1, LANES, stride=2), :] = second.T
        return carry

    lax.fori_loop(0, nodes // LANES, turn, 0, unroll=2)

    lane = iota((1, LANES), 1)
    low_half = lane < 64

    def pick_halo(side):
        def step(i, carry):
            for t in range(16):
                n = i * 16 + t
                halo_pick[side, pl.ds(2 * n, 2), :] = table[
                    pl.ds(2 * shared_ref[side, n], 2), :
                ]
            return carry

        lax.fori_loop(0, shared // 16, step, 0)
        halo_out[side, 0:shared, :] = halo_pick[side, pl.ds(0, shared, stride=2), :]
        halo_out[side, shared : shared + half, :] = halo_pick[
            side, pl.ds(1, half, stride=2), :
        ] + pltpu.roll(halo_pick[side, pl.ds(shared + 1, half, stride=2), :], 64, 1)

    def halo_copy(side):
        other = dom - 1 if side == 0 else dom + 1
        return pltpu.make_async_remote_copy(
            src_ref=halo_out.at[side],
            dst_ref=halo_in.at[1 - side],
            send_sem=halo_send.at[side],
            recv_sem=halo_recv.at[1 - side],
            device_id=(other, case),
            device_id_type=MESH,
        )

    pick_halo(0)
    pl.semaphore_wait(barrier, n_dom - 1 + groups - 1)

    @pl.when(dom > 0)
    def _():
        halo_copy(0).start()

    pick_halo(1)

    @pl.when(dom < n_dom - 1)
    def _():
        halo_copy(1).start()

    def pick_spline(i, carry):
        row = i // (slots // 16)
        col = (i % (slots // 16)) * 16
        for t in range(16):
            spline_pick[pl.ds(2 * (i * 16 + t), 2), :] = table[
                pl.ds(2 * node_ref[row, col + t], 2), :
            ]
        return carry

    lax.fori_loop(0, n_dom * slots // 16, pick_spline, 0)
    is_u = (lane >= 32) & (lane < 48)
    is_a = lane < 16

    def spline_block(j, carry):
        base = pl.multiple_of(j * 2 * slots, 2 * slots)
        first = spline_pick[pl.ds(base, slots, stride=2), :]
        second = spline_pick[pl.ds(base + 1, slots, stride=2), :]
        values = jnp.where(is_u, first, jnp.where(is_a, second, 0.0))
        coefficient = jnp.where(
            iota((1, slots), 1) < count_ref[j], weight_ref[pl.ds(j, 1), :], 0.0
        )
        onehot = jnp.where(
            iota((PANELS_DEV, slots), 0) == panel_ref[pl.ds(j, 1), :], coefficient, 0.0
        )
        wash = jnp.dot(onehot, values, precision=HIGHEST, preferred_element_type=jnp.float32)
        packed = wash[0:16]
        for g in range(1, 4):
            packed = packed + pltpu.roll(wash[16 * g : 16 * g + 16], PACK[g], 1)
        spline_out[j] = packed
        return carry

    lax.fori_loop(0, n_dom, spline_block, 0)

    def spline_copy(off):
        other = lax.rem(dom + off, n_dom)
        return pltpu.make_async_remote_copy(
            src_ref=spline_out.at[other],
            dst_ref=spline_in.at[dom],
            send_sem=spline_send.at[off],
            recv_sem=spline_recv.at[off],
            device_id=(other, case),
            device_id_type=MESH,
        )

    for off in range(1, n_dom):
        spline_copy(off).start()

    width = corners * LANES
    wide = k_ref.shape[0]
    weights = jnp.zeros((1, width), jnp.float32)
    wide_lane = iota((1, width), 1)
    for c in range(cases):
        weights = jnp.where(wide_lane % 16 == c, case_ref[c], weights)
    r = iota((width, wide), 0)
    u_dof = (r % LANES) // 16
    to_u = jnp.where(iota((width, wide), 1) == u_dof * 4 + r // LANES, 1.0, 0.0)
    q = iota((wide, width), 1)
    a_dof = ((q % LANES) // 16 + 2) % 8
    to_a = jnp.where(iota((wide, width), 0) == a_dof * 4 + q // LANES, 1.0, 0.0)
    big = jnp.dot(
        dot_lanes(to_u, k_ref[...]), to_a, precision=HIGHEST, preferred_element_type=jnp.float32
    )
    same_case = iota((width, width), 0) % 16 == iota((width, width), 1) % 16
    big = jnp.where(same_case, big * weights, 0.0)
    hi = big.astype(jnp.bfloat16)
    big_hi[...] = hi
    big_lo[...] = (big - hi.astype(jnp.float32)).astype(jnp.bfloat16)

    def unpack(side):
        base = 2 * (nodes + side * shared)
        table[pl.ds(base, shared, stride=2), :] = halo_in[side, 0:shared, :]
        both = halo_in[side, shared : shared + half, :]
        table[pl.ds(base + 1, half, stride=2), :] = jnp.where(low_half, both, 0.0)
        table[pl.ds(base + shared + 1, half, stride=2), :] = jnp.where(
            low_half, pltpu.roll(both, 64, 1), 0.0
        )

    def blank(side):
        base = 2 * (nodes + side * shared)
        table[base : base + 2 * shared, :] = jnp.zeros((2 * shared, LANES), jnp.float32)

    @pl.when(dom > 0)
    def _():
        halo_copy(1).wait_recv()
        unpack(0)

    @pl.when(dom == 0)
    def _():
        blank(0)

    @pl.when(dom < n_dom - 1)
    def _():
        halo_copy(0).wait_recv()
        unpack(1)

    @pl.when(dom == n_dom - 1)
    def _():
        blank(1)

    def pick_elements(i, carry):
        for t in range(8):
            for k in range(corners):
                e = i * 8 + t
                picked[k, pl.ds(2 * e, 2), :] = table[pl.ds(2 * conn_ref[k, e], 2), :]
        return carry

    lax.fori_loop(0, elements // 8, pick_elements, 0)
    ones = jnp.ones((8, LANES), jnp.float32)
    from_first = lane >= 96

    def energy_block(b, carry):
        base = pl.multiple_of(b * 2 * LANES, 2 * LANES)
        firsts = [picked[k, pl.ds(base, LANES, stride=2), :] for k in range(corners)]
        seconds = [picked[k, pl.ds(base + 1, LANES, stride=2), :] for k in range(corners)]
        u = jnp.concatenate(firsts, axis=1)
        u_hi = u.astype(jnp.bfloat16)
        u_lo = (u - u_hi.astype(jnp.float32)).astype(jnp.bfloat16)
        force = jnp.dot(u_hi, big_hi[...], preferred_element_type=jnp.float32)
        force = force + jnp.dot(u_lo, big_hi[...], preferred_element_type=jnp.float32)
        force = force + jnp.dot(u_hi, big_lo[...], preferred_element_type=jnp.float32)
        total = jnp.zeros((LANES, LANES), jnp.float32)
        for k in range(corners):
            adjoint = jnp.where(from_first, firsts[k], seconds[k])
            total = total + adjoint * force[:, k * LANES : (k + 1) * LANES]
        thick[pl.ds(b, 1), :] = dot_lanes(ones, total)[0:1]
        return carry

    lax.fori_loop(0, elements // LANES, energy_block, 0)

    spline_in[dom] = spline_out[dom]
    for off in range(1, n_dom):
        spline_copy(off).wait_recv()
    wash = spline_in[0]
    for s in range(1, n_dom):
        wash = wash + spline_in[s]
    product = wash * pltpu.roll(wash, LANES - 32, 1)
    spread = jnp.concatenate(
        [
            jnp.where((lane >= PACK[g]) & (lane < PACK[g] + 16), product, 0.0)
            for g in range(4)
        ],
        axis=0,
    )
    panels = dot_lanes(jnp.broadcast_to(weights[:, 0:LANES], (8, LANES)), spread)[0:1]

    message[...] = jnp.zeros_like(message)
    for z in range(groups):
        message[z, 0:share_rows, :] = thick[z * share_rows : (z + 1) * share_rows, :]
        message[z, share_rows : share_rows + 1, 0:PANELS_DEV] = panels

    def case_copy(off):
        other = lax.rem(case + off, groups)
        return pltpu.make_async_remote_copy(
            src_ref=message.at[other],
            dst_ref=arrived.at[case],
            send_sem=case_send.at[off],
            recv_sem=case_recv.at[off],
            device_id=(dom, other),
            device_id_type=MESH,
        )

    for off in range(1, groups):
        case_copy(off).start()
    arrived[case] = message[case]
    for off in range(1, groups):
        case_copy(off).wait_recv()
    total = arrived[0]
    for z in range(1, groups):
        total = total + arrived[z]
    root = math.sqrt(cases * groups)
    scaling = scale_ref[pl.ds(case * share_rows, share_rows), :]
    thick_ref[...] = -scaling * total[0:share_rows] / root
    panel_share = PANELS_DEV // groups
    shift = lax.rem(LANES - case * panel_share, LANES)
    wash_ref[...] = pltpu.roll(total, shift, 1)[share_rows : share_rows + 1] / root

    @pl.when(dom > 0)
    def _():
        halo_copy(0).wait_send()

    @pl.when(dom < n_dom - 1)
    def _():
        halo_copy(1).wait_send()

    for off in range(1, n_dom):
        spline_copy(off).wait_send()
    for off in range(1, groups):
        case_copy(off).wait_send()


def on_device(
    n_dom,
    groups,
    displacement,
    adjoint,
    stiffness_ref,
    element_scale,
    connectivity,
    shared_nodes,
    spline_node,
    spline_panel,
    spline_weight,
    spline_count,
    case_weight,
):
    cases, dof, nodes = displacement.shape
    corners, elements = connectivity.shape
    shared = shared_nodes.shape[1]
    slots = spline_node.shape[1]
    width = corners * LANES
    share_rows = elements // LANES // groups
    packed = shared + shared // 2
    f32 = jnp.float32
    vmem = pl.BlockSpec(memory_space=pltpu.VMEM)
    smem = pl.BlockSpec(memory_space=pltpu.SMEM)
    thick, panel = pl.pallas_call(
        functools.partial(kernel, n_dom, groups),
        out_shape=(
            jax.ShapeDtypeStruct((share_rows, LANES), f32),
            jax.ShapeDtypeStruct((1, LANES), f32),
        ),
        in_specs=[vmem] * 6 + [smem] * 5,
        out_specs=(vmem, vmem),
        scratch_shapes=[
            pltpu.VMEM((2 * (nodes + 2 * shared), LANES), f32),
            pltpu.VMEM((corners, 2 * elements, LANES), f32),
            pltpu.VMEM((2, 2 * shared, LANES), f32),
            pltpu.VMEM((2, packed, LANES), f32),
            pltpu.VMEM((2, packed, LANES), f32),
            pltpu.VMEM((2 * n_dom * slots, LANES), f32),
            pltpu.VMEM((n_dom, 16, LANES), f32),
            pltpu.VMEM((n_dom, 16, LANES), f32),
            pltpu.VMEM((width, width), jnp.bfloat16),
            pltpu.VMEM((width, width), jnp.bfloat16),
            pltpu.VMEM((elements // LANES, LANES), f32),
            pltpu.VMEM((groups, 8, LANES), f32),
            pltpu.VMEM((groups, 8, LANES), f32),
            pltpu.SemaphoreType.DMA((2,)),
            pltpu.SemaphoreType.DMA((2,)),
            pltpu.SemaphoreType.DMA((n_dom,)),
            pltpu.SemaphoreType.DMA((n_dom,)),
            pltpu.SemaphoreType.DMA((groups,)),
            pltpu.SemaphoreType.DMA((groups,)),
        ],
        compiler_params=pltpu.CompilerParams(
            collective_id=0, has_side_effects=True, vmem_limit_bytes=48 * 2**20
        ),
    )(
        jnp.transpose(displacement, (1, 0, 2)).reshape(dof * cases, nodes),
        jnp.transpose(adjoint, (1, 0, 2)).reshape(dof * cases, nodes),
        stiffness_ref,
        element_scale.reshape(elements // LANES, LANES),
        spline_panel,
        spline_weight,
        connectivity,
        shared_nodes,
        spline_node,
        spline_count,
        case_weight,
    )
    return thick.reshape(share_rows * LANES), panel[0, : PANELS_DEV // groups]


def solution(mesh):
    return jax.shard_map(
        functools.partial(on_device, mesh.shape["dom"], mesh.shape["case"]),
        mesh=mesh,
        in_specs=(
            P("case", None, "dom"),
            P("case", None, "dom"),
            P(),
            P("dom"),
            P(None, "dom"),
            P(None, "dom"),
            P("dom", None),
            P("dom", None),
            P("dom", None),
            P("dom"),
            P("case"),
        ),
        out_specs=(P(("dom", "case")), P(("dom", "case"))),
        check_vma=False,
    )
```

time: 159 us -> 46.1 us (0.29)
  the two profiles are of different devices: /device:TPU:0 before, /device:TPU:4 now
where the time goes in v1:
time: 46.1 us; the launch traced here: 45.6 us
  Pallas kernels  34.8 us (75%)
  local copies, waits for them, and re-layouts  10 us (22%)
  between operations  0.66 us (1%)
    pallas_call x1, Pallas kernels, on_device(): pl.pallas_call(functools.partial(kernel, n_dom, groups), out_shape=(jax.S...  34.8 us
    unnamed x23, local copies, waits for them, and re-layouts  9.54 us

profile of v1, /device:TPU:4, one launch (start us, length us, event | category | flops | bytes accessed | tf_op | source)
XLA Modules:
  0.0 45.6 jit_solution(3148370709489784846)
XLA Ops:
  0.6 0.0 copy-start
  0.6 1.4 %copy-done = f32[16,6,4096]{2,0,1:T(8,128)S(1)} copy-done((f32[16,6,4096]{2,0,1:T(8,128)S(1)}, f32[16,6,4096]{2,0,1:T(8,128)}, u32[]{:S(2)}) %copy-start) | copy-done | bytes 1572888
  2.0 0.0 copy-start.1
  2.0 1.4 %copy-done.1 = f32[16,6,4096]{2,0,1:T(8,128)S(1)} copy-done((f32[16,6,4096]{2,0,1:T(8,128)S(1)}, f32[16,6,4096]{2,0,1:T(8,128)}, u32[]{:S(2)}) %copy-start.1) | copy-done | bytes 1572888
  3.5 0.0 copy-start.2
  3.5 0.7 %copy-done.2 = s32[4,1024]{1,0:T(4,128)S(1)} copy-done((s32[4,1024]{1,0:T(4,128)S(1)}, s32[4,1024]{1,0:T(4,128)}, u32[]{:S(2)}) %copy-start.2) | copy-done | bytes 16408
  4.2 0.0 copy-start.3
  4.2 0.7 %copy-done.3 = f32[24,24]{1,0:T(8,128)S(1)} copy-done((f32[24,24]{1,0:T(8,128)S(1)}, f32[24,24]{1,0:T(8,128)}, u32[]{:S(2)}) %copy-start.3) | copy-done | bytes 2328
  4.9 0.0 copy-start.4
  4.9 0.7 %copy-done.4 = f32[1024]{0:T(1024)S(1)} copy-done((f32[1024]{0:T(1024)S(1)}, f32[1024]{0:T(1024)}, u32[]{:S(2)}) %copy-start.4) | copy-done | bytes 4120
  5.6 0.0 copy-start.5
  5.6 0.7 %copy-done.5 = s32[8,128]{1,0:T(8,128)S(1)} copy-done((s32[8,128]{1,0:T(8,128)S(1)}, s32[8,128]{1,0:T(8,128)}, u32[]{:S(2)}) %copy-start.5) | copy-done | bytes 4120
  6.3 0.0 copy-start.6
  6.3 0.7 %copy-done.6 = f32[8,128]{1,0:T(8,128)S(1)} copy-done((f32[8,128]{1,0:T(8,128)S(1)}, f32[8,128]{1,0:T(8,128)}, u32[]{:S(2)}) %copy-start.6) | copy-done | bytes 4120
  6.9 0.0 copy-start.7
  6.9 0.7 %copy-done.7 = s32[2,512]{1,0:T(2,128)S(1)} copy-done((s32[2,512]{1,0:T(2,128)S(1)}, s32[2,512]{1,0:T(2,128)}, u32[]{:S(2)}) %copy-start.7) | copy-done | bytes 4120
  7.6 0.0 copy-start.8
  7.6 0.7 %copy-done.8 = s32[8,128]{1,0:T(8,128)S(1)} copy-done((s32[8,128]{1,0:T(8,128)S(1)}, s32[8,128]{1,0:T(8,128)}, u32[]{:S(2)}) %copy-start.8) | copy-done | bytes 4120
  8.3 0.0 copy-start.9
  8.3 0.7 %copy-done.9 = s32[8]{0:T(128)S(1)} copy-done((s32[8]{0:T(128)S(1)}, s32[8]{0:T(128)}, u32[]{:S(2)}) %copy-start.9) | copy-done | bytes 56
  9.0 0.0 copy-start.10
  9.0 0.7 %copy-done.10 = f32[16]{0:T(128)S(1)} copy-done((f32[16]{0:T(128)S(1)}, f32[16]{0:T(128)}, u32[]{:S(2)}) %copy-start.10) | copy-done | bytes 88
  9.6 34.8 %shard_map.122 = (f32[2,128]{1,0:T(2,128)S(1)}, f32[1,128]{1,0:T(1,128)S(1)}) custom-call(f32[96,4096]{1,0:T(8,128)S(1)} %bitcast.10, f32[96,4096]{1,0:T(8,128)S(1)} %bitcast.11, f32[24,24]{1,0:T(8,128)S(1)} %copy-done.3, f32[8,128]{1,0:T(8,128)S(1)} %bitcast.12, s32[8,128]{1,0:T(8,128)S(1)} %copy-done.5, f32[8,128]{1,0:T(8,128)S(1)} %copy-done.6, ...), custom_call_target="tpu_custom_call" | custom-call | tf_op jit(solution)/shard_map/pallas_call | solution.py:355
  44.5 0.5 %slice_bitcast_fusion = f32[16]{0:T(128)} fusion(f32[1,128]{1,0:T(1,128)S(1)} %get-tuple-element.5), kind=kLoop, calls=%fused_computation | loop fusion | bytes 128 | tf_op jit(solution)/shard_map/squeeze | solution.py:400
  45.0 0.6 %copy.14 = f32[256]{0:T(256)} copy(f32[256]{0:T(256)S(1)} %bitcast.13) | data formatting | bytes 2048
Async XLA Ops:
  0.6 1.4 %copy-start = (f32[16,6,4096]{2,0,1:T(8,128)S(1)}, f32[16,6,4096]{2,0,1:T(8,128)}, u32[]{:S(2)}) copy-start(f32[16,6,4096]{2,0,1:T(8,128)} %param.11) | copy-start | bytes 4718596
  2.0 1.4 %copy-start.1 = (f32[16,6,4096]{2,0,1:T(8,128)S(1)}, f32[16,6,4096]{2,0,1:T(8,128)}, u32[]{:S(2)}) copy-start(f32[16,6,4096]{2,0,1:T(8,128)} %param.12) | copy-start | bytes 4718596
  3.5 0.7 %copy-start.2 = (s32[4,1024]{1,0:T(4,128)S(1)}, s32[4,1024]{1,0:T(4,128)}, u32[]{:S(2)}) copy-start(s32[4,1024]{1,0:T(4,128)} %conn_ref.1) | copy-start | bytes 49156
  4.2 0.7 %copy-start.3 = (f32[24,24]{1,0:T(8,128)S(1)}, f32[24,24]{1,0:T(8,128)}, u32[]{:S(2)}) copy-start(f32[24,24]{1,0:T(8,128)} %k_ref.1) | copy-start | bytes 6916
  4.9 0.7 %copy-start.4 = (f32[1024]{0:T(1024)S(1)}, f32[1024]{0:T(1024)}, u32[]{:S(2)}) copy-start(f32[1024]{0:T(1024)} %param.14) | copy-start | bytes 12292
  5.6 0.7 %copy-start.5 = (s32[8,128]{1,0:T(8,128)S(1)}, s32[8,128]{1,0:T(8,128)}, u32[]{:S(2)}) copy-start(s32[8,128]{1,0:T(8,128)} %panel_ref.1) | copy-start | bytes 12292
  6.3 0.7 %copy-start.6 = (f32[8,128]{1,0:T(8,128)S(1)}, f32[8,128]{1,0:T(8,128)}, u32[]{:S(2)}) copy-start(f32[8,128]{1,0:T(8,128)} %weight_ref.1) | copy-start | bytes 12292
  6.9 0.7 %copy-start.7 = (s32[2,512]{1,0:T(2,128)S(1)}, s32[2,512]{1,0:T(2,128)}, u32[]{:S(2)}) copy-start(s32[2,512]{1,0:T(2,128)} %shared_ref.1) | copy-start | bytes 12292
  7.6 0.7 %copy-start.8 = (s32[8,128]{1,0:T(8,128)S(1)}, s32[8,128]{1,0:T(8,128)}, u32[]{:S(2)}) copy-start(s32[8,128]{1,0:T(8,128)} %node_ref.1) | copy-start | bytes 12292
  8.3 0.7 %copy-start.9 = (s32[8]{0:T(128)S(1)}, s32[8]{0:T(128)}, u32[]{:S(2)}) copy-start(s32[8]{0:T(128)} %count_ref.1) | copy-start | bytes 100
  9.0 0.7 %copy-start.10 = (f32[16]{0:T(128)S(1)}, f32[16]{0:T(128)}, u32[]{:S(2)}) copy-start(f32[16]{0:T(128)} %case_ref.1) | copy-start | bytes 196

commit v2 on v1

--- a/solution.py
+++ b/solution.py
@@ -13,6 +13,7 @@
 HIGHEST = lax.Precision.HIGHEST
 MESH = pl.DeviceIdType.MESH
 PACK = (0, 16, 64, 80)
+LOADS = 4
 
 
 def iota(shape, dim):
@@ -28,47 +29,82 @@
 def kernel(
     n_dom,
     groups,
-    u_ref,
-    a_ref,
-    k_ref,
-    scale_ref,
-    panel_ref,
-    weight_ref,
-    conn_ref,
-    shared_ref,
-    node_ref,
-    count_ref,
-    case_ref,
-    thick_ref,
-    wash_ref,
-    table,
-    picked,
-    halo_pick,
-    halo_out,
-    halo_in,
-    spline_pick,
-    spline_out,
-    spline_in,
-    big_hi,
-    big_lo,
-    thick,
-    message,
-    arrived,
-    halo_send,
-    halo_recv,
-    spline_send,
-    spline_recv,
-    case_send,
-    case_recv,
+    u_hbm,
+    a_hbm,
+    *refs,
 ):
+    smalls, refs = refs[:9], refs[9:]
+    (thick_ref, wash_ref, u_ref, a_ref), refs = refs[:4], refs[4:]
+    held, refs = refs[:9], refs[9:]
+    (
+        k_ref,
+        scale_ref,
+        panel_ref,
+        weight_ref,
+        conn_ref,
+        shared_ref,
+        node_ref,
+        count_ref,
+        case_ref,
+    ) = held
+    (
+        table,
+        picked,
+        halo_pick,
+        halo_out,
+        halo_in,
+        spline_pick,
+        spline_out,
+        spline_in,
+        big_hi,
+        big_lo,
+        thick,
+        message,
+        arrived,
+        halo_send,
+        halo_recv,
+        spline_send,
+        spline_recv,
+        case_send,
+        case_recv,
+        load_sem,
+        small_sem,
+    ) = refs
     cases = case_ref.shape[0]
     nodes = u_ref.shape[1]
-    corners, elements = conn_ref.shape
-    shared = shared_ref.shape[1]
-    slots = node_ref.shape[1]
+    corners, elements = smalls[4].shape
+    shared = smalls[5].shape[1]
+    slots = smalls[6].shape[1]
     half = shared // 2
     share_rows = elements // LANES // groups
     dom, case = lax.axis_index("dom"), lax.axis_index("case")
+
+    loads = []
+    for part in range(LOADS):
+        cols = pl.ds(part * (nodes // LOADS), nodes // LOADS)
+        pair = [
+            pltpu.make_async_copy(
+                source.at[:, cols], target.at[:, cols], load_sem.at[which, part]
+            )
+            for which, (source, target) in enumerate(((u_hbm, u_ref), (a_hbm, a_ref)))
+        ]
+        for copy in pair:
+            copy.start()
+        loads.append(pair)
+    small_pairs = []
+    for source, target in zip(smalls, held):
+        if source.shape == target.shape:
+            small_pairs.append((source, target))
+        else:
+            size = source.shape[1]
+            for row in range(source.shape[0]):
+                small_pairs.append((source.at[row], target.at[pl.ds(row * size, size)]))
+    small_loads = [
+        pltpu.make_async_copy(source, target, small_sem.at[i])
+        for i, (source, target) in enumerate(small_pairs)
+    ]
+    for copy in small_loads:
+        copy.start()
 
     barrier = pltpu.get_barrier_semaphore()
     for off in range(1, n_dom):
@@ -93,7 +129,13 @@
         table[pl.ds(start + 1, LANES, stride=2), :] = second.T
         return carry
 
-    lax.fori_loop(0, nodes // LANES, turn, 0, unroll=2)
+    per_load = nodes // LANES // LOADS
+    for part, pair in enumerate(loads):
+        for copy in pair:
+            copy.wait()
+        lax.fori_loop(part * per_load, (part + 1) * per_load, turn, 0, unroll=8)
+    for copy in small_loads:
+        copy.wait()
 
     lane = iota((1, LANES), 1)
     low_half = lane < 64
@@ -103,7 +145,7 @@
             for t in range(16):
                 n = i * 16 + t
                 halo_pick[side, pl.ds(2 * n, 2), :] = table[
-                    pl.ds(2 * shared_ref[side, n], 2), :
+                    pl.ds(2 * shared_ref[side * shared + n], 2), :
                 ]
             return carry
 
@@ -138,11 +180,9 @@
         halo_copy(1).start()
 
     def pick_spline(i, carry):
-        row = i // (slots // 16)
-        col = (i % (slots // 16)) * 16
         for t in range(16):
             spline_pick[pl.ds(2 * (i * 16 + t), 2), :] = table[
-                pl.ds(2 * node_ref[row, col + t], 2), :
+                pl.ds(2 * node_ref[i * 16 + t], 2), :
             ]
         return carry
 
@@ -240,31 +280,40 @@
         for t in range(8):
             for k in range(corners):
                 e = i * 8 + t
-                picked[k, pl.ds(2 * e, 2), :] = table[pl.ds(2 * conn_ref[k, e], 2), :]
+                picked[k, pl.ds(2 * e, 2), :] = table[pl.ds(2 * conn_ref[k * elements + e], 2), :]
         return carry
 
     lax.fori_loop(0, elements // 8, pick_elements, 0)
-    ones = jnp.ones((8, LANES), jnp.float32)
+    ones = jnp.ones((8, LANES), jnp.bfloat16)
     from_first = lane >= 96
-
-    def energy_block(b, carry):
-        base = pl.multiple_of(b * 2 * LANES, 2 * LANES)
-        firsts = [picked[k, pl.ds(base, LANES, stride=2), :] for k in range(corners)]
-        seconds = [picked[k, pl.ds(base + 1, LANES, stride=2), :] for k in range(corners)]
-        u = jnp.concatenate(firsts, axis=1)
-        u_hi = u.astype(jnp.bfloat16)
-        u_lo = (u - u_hi.astype(jnp.float32)).astype(jnp.bfloat16)
+    block = min(512, elements)
+
+    def split(x):
+        high = x.astype(jnp.bfloat16)
+        return high, (x - high.astype(jnp.float32)).astype(jnp.bfloat16)
+
+    def lane_sum(x):
+        return lax.dot_general(
+            ones, x, (((1,), (1,)), ((), ())), preferred_element_type=jnp.float32
+        )
+
+    for b in range(elements // block):
+        base = 2 * b * block
+        firsts = [picked[k, pl.ds(base, block, stride=2), :] for k in range(corners)]
+        seconds = [picked[k, pl.ds(base + 1, block, stride=2), :] for k in range(corners)]
+        u_hi, u_lo = split(jnp.concatenate(firsts, axis=1))
         force = jnp.dot(u_hi, big_hi[...], preferred_element_type=jnp.float32)
         force = force + jnp.dot(u_lo, big_hi[...], preferred_element_type=jnp.float32)
         force = force + jnp.dot(u_hi, big_lo[...], preferred_element_type=jnp.float32)
-        total = jnp.zeros((LANES, LANES), jnp.float32)
+        total = jnp.zeros((block, LANES), jnp.float32)
         for k in range(corners):
             adjoint = jnp.where(from_first, firsts[k], seconds[k])
             total = total + adjoint * force[:, k * LANES : (k + 1) * LANES]
-        thick[pl.ds(b, 1), :] = dot_lanes(ones, total)[0:1]
-        return carry
-
-    lax.fori_loop(0, elements // LANES, energy_block, 0)
+        total_hi, total_lo = split(total)
+        row = (lane_sum(total_hi) + lane_sum(total_lo))[0:1]
+        for part in range(block // LANES):
+            at = b * (block // LANES) + part
+            thick[at : at + 1, :] = row[:, part * LANES : (part + 1) * LANES]
 
     spline_in[dom] = spline_out[dom]
     for off in range(1, n_dom):
@@ -351,16 +400,27 @@
     packed = shared + shared // 2
     f32 = jnp.float32
     vmem = pl.BlockSpec(memory_space=pltpu.VMEM)
-    smem = pl.BlockSpec(memory_space=pltpu.SMEM)
+    hbm = pl.BlockSpec(memory_space=pltpu.HBM)
     thick, panel = pl.pallas_call(
         functools.partial(kernel, n_dom, groups),
         out_shape=(
             jax.ShapeDtypeStruct((share_rows, LANES), f32),
             jax.ShapeDtypeStruct((1, LANES), f32),
         ),
-        in_specs=[vmem] * 6 + [smem] * 5,
+        in_specs=[hbm] * 11,
         out_specs=(vmem, vmem),
         scratch_shapes=[
+            pltpu.VMEM((dof * cases, nodes), f32),
+            pltpu.VMEM((dof * cases, nodes), f32),
+            pltpu.VMEM(stiffness_ref.shape, f32),
+            pltpu.VMEM((elements // LANES, LANES), f32),
+            pltpu.VMEM(spline_panel.shape, jnp.int32),
+            pltpu.VMEM(spline_weight.shape, f32),
+            pltpu.SMEM((corners * elements,), jnp.int32),
+            pltpu.SMEM((2 * shared,), jnp.int32),
+            pltpu.SMEM((n_dom * slots,), jnp.int32),
+            pltpu.SMEM(spline_count.shape, jnp.int32),
+            pltpu.SMEM(case_weight.shape, f32),
             pltpu.VMEM((2 * (nodes + 2 * shared), LANES), f32),
             pltpu.VMEM((corners, 2 * elements, LANES), f32),
             pltpu.VMEM((2, 2 * shared, LANES), f32),
@@ -380,9 +440,11 @@
             pltpu.SemaphoreType.DMA((n_dom,)),
             pltpu.SemaphoreType.DMA((groups,)),
             pltpu.SemaphoreType.DMA((groups,)),
+            pltpu.SemaphoreType.DMA((2, LOADS)),
+            pltpu.SemaphoreType.DMA((6 + corners + 2 + n_dom,)),
         ],
         compiler_params=pltpu.CompilerParams(
-            collective_id=0, has_side_effects=True, vmem_limit_bytes=48 * 2**20
+            collective_id=0, has_side_effects=True, vmem_limit_bytes=62 * 2**20
         ),
     )(
         jnp.transpose(displacement, (1, 0, 2)).reshape(dof * cases, nodes),

time: 46.1 us -> 33.6 us (0.73)
  the two profiles are of different devices: /device:TPU:4 before, /device:TPU:1 now
where the time goes in v2:
time: 33.6 us; the launch traced here: 33.4 us
  Pallas kernels  30.4 us (90%)
  local copies, waits for them, and re-layouts  2.36 us (7%)
  between operations  0.64 us (2%)
    pallas_call x1, Pallas kernels, on_device(): pl.pallas_call(functools.partial(kernel, n_dom, groups), out_shape=(jax.S...  30.4 us
    unnamed x1, local copies, waits for them, and re-layouts  1.22 us
    squeeze x1, local copies, waits for them, and re-layouts, on_device(): return (thick.reshape(share_rows * LANES), panel[0, :PANELS_DEV // groups])  1.14 us

profile of v2, /device:TPU:1, one launch (start us, length us, event | category | flops | bytes accessed | tf_op | source)
XLA Modules:
  0.0 33.4 jit_solution(5491799978085443199)
XLA Ops:
  0.6 30.4 %shard_map.122 = (f32[2,128]{1,0:T(2,128)}, f32[1,128]{1,0:T(1,128)}) custom-call(f32[96,4096]{1,0:T(8,128)} %bitcast.10, f32[96,4096]{1,0:T(8,128)} %bitcast.11, f32[24,24]{1,0:T(8,128)} %refs_0_.1, f32[8,128]{1,0:T(8,128)} %bitcast.12, s32[8,128]{1,0:T(8,128)} %refs_2_.1, f32[8,128]{1,0:T(8,128)} %refs_3_.1, s32[4,1024]{1,0:T(4,128)} %refs_4_.1, ...), custom_call_target="tpu_custom_call" | custom-call | tf_op jit(solution)/shard_map/pallas_call | solution.py:404
  31.0 1.1 %slice_bitcast_fusion = f32[16]{0:T(128)} fusion(f32[1,128]{1,0:T(1,128)} %get-tuple-element.5), kind=kLoop, calls=%fused_computation | loop fusion | bytes 128 | tf_op jit(solution)/shard_map/squeeze | solution.py:462
  32.1 1.2 %copy.14 = f32[256]{0:T(256)} copy(f32[256]{0:T(256)} %bitcast.13) | data formatting | bytes 2048

commit v3 on v2

--- a/solution.py
+++ b/solution.py
@@ -14,6 +14,7 @@
 MESH = pl.DeviceIdType.MESH
 PACK = (0, 16, 64, 80)
 LOADS = 4
+PARTS = 4
 
 
 def iota(shape, dim):
@@ -36,6 +37,7 @@
     smalls, refs = refs[:9], refs[9:]
     (thick_ref, wash_ref, u_ref, a_ref), refs = refs[:4], refs[4:]
     held, refs = refs[:9], refs[9:]
+    staged, refs = dict(zip((4, 5, 6), refs[:3])), refs[3:]
     (
         k_ref,
         scale_ref,
@@ -69,13 +71,15 @@
         case_recv,
         load_sem,
         small_sem,
+        index_sem,
     ) = refs
     cases = case_ref.shape[0]
     nodes = u_ref.shape[1]
     corners, elements = smalls[4].shape
     shared = smalls[5].shape[1]
     slots = smalls[6].shape[1]
-    half = shared // 2
+    part_nodes = shared // PARTS
+    half = part_nodes // 2
     share_rows = elements // LANES // groups
     dom, case = lax.axis_index("dom"), lax.axis_index("case")
 
@@ -91,17 +95,9 @@
         for copy in pair:
             copy.start()
         loads.append(pair)
-    small_pairs = []
-    for source, target in zip(smalls, held):
-        if source.shape == target.shape:
-            small_pairs.append((source, target))
-        else:
-            size = source.shape[1]
-            for row in range(source.shape[0]):
-                small_pairs.append((source.at[row], target.at[pl.ds(row * size, size)]))
     small_loads = [
-        pltpu.make_async_copy(source, target, small_sem.at[i])
-        for i, (source, target) in enumerate(small_pairs)
+        pltpu.make_async_copy(source, staged.get(i, target), small_sem.at[i])
+        for i, (source, target) in enumerate(zip(smalls, held))
     ]
     for copy in small_loads:
         copy.start()
@@ -129,60 +125,83 @@
         table[pl.ds(start + 1, LANES, stride=2), :] = second.T
         return carry
 
+    index_loads = []
+    for i in (4, 5, 6):
+        small_loads[i].wait()
+        staged[i][...] = staged[i][...] * 2
+        size = smalls[i].shape[1]
+        for row in range(smalls[i].shape[0]):
+            copy = pltpu.make_async_copy(
+                staged[i].at[row],
+                held[i].at[pl.ds(row * size, size)],
+                index_sem.at[len(index_loads)],
+            )
+            copy.start()
+            index_loads.append(copy)
     per_load = nodes // LANES // LOADS
     for part, pair in enumerate(loads):
         for copy in pair:
             copy.wait()
         lax.fori_loop(part * per_load, (part + 1) * per_load, turn, 0, unroll=8)
-    for copy in small_loads:
+    for i, copy in enumerate(small_loads):
+        if i not in staged:
+            copy.wait()
+    for copy in index_loads:
         copy.wait()
 
     lane = iota((1, LANES), 1)
     low_half = lane < 64
 
-    def pick_halo(side):
+    def pick_halo(side, part):
         def step(i, carry):
             for t in range(16):
-                n = i * 16 + t
+                n = part * part_nodes + i * 16 + t
                 halo_pick[side, pl.ds(2 * n, 2), :] = table[
-                    pl.ds(2 * shared_ref[side * shared + n], 2), :
+                    pl.ds(shared_ref[side * shared + n], 2), :
                 ]
             return carry
 
-        lax.fori_loop(0, shared // 16, step, 0)
-        halo_out[side, 0:shared, :] = halo_pick[side, pl.ds(0, shared, stride=2), :]
-        halo_out[side, shared : shared + half, :] = halo_pick[
-            side, pl.ds(1, half, stride=2), :
-        ] + pltpu.roll(halo_pick[side, pl.ds(shared + 1, half, stride=2), :], 64, 1)
-
-    def halo_copy(side):
+        lax.fori_loop(0, part_nodes // 16, step, 0)
+        base = 2 * part * part_nodes
+        halo_out[side, part, 0:part_nodes, :] = halo_pick[
+            side, pl.ds(base, part_nodes, stride=2), :
+        ]
+        halo_out[side, part, part_nodes : part_nodes + half, :] = halo_pick[
+            side, pl.ds(base + 1, half, stride=2), :
+        ] + pltpu.roll(
+            halo_pick[side, pl.ds(base + part_nodes + 1, half, stride=2), :], 64, 1
+        )
+
+    def halo_copy(side, part):
         other = dom - 1 if side == 0 else dom + 1
         return pltpu.make_async_remote_copy(
-            src_ref=halo_out.at[side],
-            dst_ref=halo_in.at[1 - side],
-            send_sem=halo_send.at[side],
-            recv_sem=halo_recv.at[1 - side],
+            src_ref=halo_out.at[side, part],
+            dst_ref=halo_in.at[1 - side, part],
+            send_sem=halo_send.at[side, part],
+            recv_sem=halo_recv.at[1 - side, part],
             device_id=(other, case),
             device_id_type=MESH,
         )
 
-    pick_halo(0)
-    pl.semaphore_wait(barrier, n_dom - 1 + groups - 1)
-
-    @pl.when(dom > 0)
-    def _():
-        halo_copy(0).start()
-
-    pick_halo(1)
-
-    @pl.when(dom < n_dom - 1)
-    def _():
-        halo_copy(1).start()
+    for part in range(PARTS):
+        pick_halo(0, part)
+        if part == 0:
+            pl.semaphore_wait(barrier, n_dom - 1 + groups - 1)
+
+        @pl.when(dom > 0)
+        def _():
+            halo_copy(0, part).start()
+
+        pick_halo(1, part)
+
+        @pl.when(dom < n_dom - 1)
+        def _():
+            halo_copy(1, part).start()
 
     def pick_spline(i, carry):
         for t in range(16):
             spline_pick[pl.ds(2 * (i * 16 + t), 2), :] = table[
-                pl.ds(2 * node_ref[i * 16 + t], 2), :
+                pl.ds(node_ref[i * 16 + t], 2), :
             ]
         return carry
 
@@ -245,12 +264,12 @@
     big_hi[...] = hi
     big_lo[...] = (big - hi.astype(jnp.float32)).astype(jnp.bfloat16)
 
-    def unpack(side):
-        base = 2 * (nodes + side * shared)
-        table[pl.ds(base, shared, stride=2), :] = halo_in[side, 0:shared, :]
-        both = halo_in[side, shared : shared + half, :]
+    def unpack(side, part):
+        base = 2 * (nodes + side * shared + part * part_nodes)
+        table[pl.ds(base, part_nodes, stride=2), :] = halo_in[side, part, 0:part_nodes, :]
+        both = halo_in[side, part, part_nodes : part_nodes + half, :]
         table[pl.ds(base + 1, half, stride=2), :] = jnp.where(low_half, both, 0.0)
-        table[pl.ds(base + shared + 1, half, stride=2), :] = jnp.where(
+        table[pl.ds(base + part_nodes + 1, half, stride=2), :] = jnp.where(
             low_half, pltpu.roll(both, 64, 1), 0.0
         )
 
@@ -258,29 +277,31 @@
         base = 2 * (nodes + side * shared)
         table[base : base + 2 * shared, :] = jnp.zeros((2 * shared, LANES), jnp.float32)
 
-    @pl.when(dom > 0)
-    def _():
-        halo_copy(1).wait_recv()
-        unpack(0)
-
     @pl.when(dom == 0)
     def _():
         blank(0)
 
-    @pl.when(dom < n_dom - 1)
-    def _():
-        halo_copy(0).wait_recv()
-        unpack(1)
-
     @pl.when(dom == n_dom - 1)
     def _():
         blank(1)
+
+    for part in range(PARTS):
+
+        @pl.when(dom > 0)
+        def _():
+            halo_copy(1, part).wait_recv()
+            unpack(0, part)
+
+        @pl.when(dom < n_dom - 1)
+        def _():
+            halo_copy(0, part).wait_recv()
+            unpack(1, part)
 
     def pick_elements(i, carry):
         for t in range(8):
             for k in range(corners):
                 e = i * 8 + t
-                picked[k, pl.ds(2 * e, 2), :] = table[pl.ds(2 * conn_ref[k * elements + e], 2), :]
+                picked[k, pl.ds(2 * e, 2), :] = table[pl.ds(conn_ref[k * elements + e], 2), :]
         return carry
 
     lax.fori_loop(0, elements // 8, pick_elements, 0)
@@ -364,11 +385,13 @@
 
     @pl.when(dom > 0)
     def _():
-        halo_copy(0).wait_send()
+        for part in range(PARTS):
+            halo_copy(0, part).wait_send()
 
     @pl.when(dom < n_dom - 1)
     def _():
-        halo_copy(1).wait_send()
+        for part in range(PARTS):
+            halo_copy(1, part).wait_send()
 
     for off in range(1, n_dom):
         spline_copy(off).wait_send()
@@ -397,7 +420,7 @@
     slots = spline_node.shape[1]
     width = corners * LANES
     share_rows = elements // LANES // groups
-    packed = shared + shared // 2
+    packed = (shared + shared // 2) // PARTS
     f32 = jnp.float32
     vmem = pl.BlockSpec(memory_space=pltpu.VMEM)
     hbm = pl.BlockSpec(memory_space=pltpu.HBM)
@@ -421,11 +444,14 @@
             pltpu.SMEM((n_dom * slots,), jnp.int32),
             pltpu.SMEM(spline_count.shape, jnp.int32),
             pltpu.SMEM(case_weight.shape, f32),
+            pltpu.VMEM(connectivity.shape, jnp.int32),
+            pltpu.VMEM(shared_nodes.shape, jnp.int32),
+            pltpu.VMEM(spline_node.shape, jnp.int32),
             pltpu.VMEM((2 * (nodes + 2 * shared), LANES), f32),
             pltpu.VMEM((corners, 2 * elements, LANES), f32),
             pltpu.VMEM((2, 2 * shared, LANES), f32),
-            pltpu.VMEM((2, packed, LANES), f32),
-            pltpu.VMEM((2, packed, LANES), f32),
+            pltpu.VMEM((2, PARTS, packed, LANES), f32),
+            pltpu.VMEM((2, PARTS, packed, LANES), f32),
             pltpu.VMEM((2 * n_dom * slots, LANES), f32),
             pltpu.VMEM((n_dom, 16, LANES), f32),
             pltpu.VMEM((n_dom, 16, LANES), f32),
@@ -434,14 +460,15 @@
             pltpu.VMEM((elements // LANES, LANES), f32),
             pltpu.VMEM((groups, 8, LANES), f32),
             pltpu.VMEM((groups, 8, LANES), f32),
-            pltpu.SemaphoreType.DMA((2,)),
-            pltpu.SemaphoreType.DMA((2,)),
+            pltpu.SemaphoreType.DMA((2, PARTS)),
+            pltpu.SemaphoreType.DMA((2, PARTS)),
             pltpu.SemaphoreType.DMA((n_dom,)),
             pltpu.SemaphoreType.DMA((n_dom,)),
             pltpu.SemaphoreType.DMA((groups,)),
             pltpu.SemaphoreType.DMA((groups,)),
             pltpu.SemaphoreType.DMA((2, LOADS)),
-            pltpu.SemaphoreType.DMA((6 + corners + 2 + n_dom,)),
+            pltpu.SemaphoreType.DMA((9,)),
+            pltpu.SemaphoreType.DMA((corners + 2 + n_dom,)),
         ],
         compiler_params=pltpu.CompilerParams(
             collective_id=0, has_side_effects=True, vmem_limit_bytes=62 * 2**20

time: 33.6 us -> 32.2 us (0.958)
  Pallas kernels: 30.4 us -> 29 us
    pallas_call x1, Pallas kernels: 30.4 us -> 29 us  [on_device(): pl.pallas_call(functools.partial(kernel, n_dom, groups), out_shape=(jax.S...]
where the time goes in v3:
time: 32.2 us; the launch traced here: 32 us
  Pallas kernels  29 us (90%)
  local copies, waits for them, and re-layouts  2.36 us (7%)
  between operations  0.64 us (2%)
    pallas_call x1, Pallas kernels, on_device(): pl.pallas_call(functools.partial(kernel, n_dom, groups), out_shape=(jax.S...  29 us
    unnamed x1, local copies, waits for them, and re-layouts  1.22 us
    squeeze x1, local copies, waits for them, and re-layouts, on_device(): return (thick.reshape(share_rows * LANES), panel[0, :PANELS_DEV // groups])  1.14 us

profile of v3, /device:TPU:1, one launch (start us, length us, event | category | flops | bytes accessed | tf_op | source)
XLA Modules:
  0.0 32.0 jit_solution(4592964354085117571)
XLA Ops:
  0.6 29.0 %shard_map.122 = (f32[2,128]{1,0:T(2,128)}, f32[1,128]{1,0:T(1,128)}) custom-call(f32[96,4096]{1,0:T(8,128)} %bitcast.10, f32[96,4096]{1,0:T(8,128)} %bitcast.11, f32[24,24]{1,0:T(8,128)} %refs_0_.1, f32[8,128]{1,0:T(8,128)} %bitcast.12, s32[8,128]{1,0:T(8,128)} %refs_2_.1, f32[8,128]{1,0:T(8,128)} %refs_3_.1, s32[4,1024]{1,0:T(4,128)} %refs_4_.1, ...), custom_call_target="tpu_custom_call" | custom-call | tf_op jit(solution)/shard_map/pallas_call | solution.py:427
  29.6 1.1 %slice_bitcast_fusion = f32[16]{0:T(128)} fusion(f32[1,128]{1,0:T(1,128)} %get-tuple-element.5), kind=kLoop, calls=%fused_computation | loop fusion | bytes 128 | tf_op jit(solution)/shard_map/squeeze | solution.py:489
  30.8 1.2 %copy.14 = f32[256]{0:T(256)} copy(f32[256]{0:T(256)} %bitcast.13) | data formatting | bytes 2048

commit v4 on v3

--- a/solution.py
+++ b/solution.py
@@ -35,7 +35,7 @@
     *refs,
 ):
     smalls, refs = refs[:9], refs[9:]
-    (thick_ref, wash_ref, u_ref, a_ref), refs = refs[:4], refs[4:]
+    (out_ref, u_ref, a_ref), refs = refs[:3], refs[3:]
     held, refs = refs[:9], refs[9:]
     staged, refs = dict(zip((4, 5, 6), refs[:3])), refs[3:]
     (
@@ -298,13 +298,13 @@
             unpack(1, part)
 
     def pick_elements(i, carry):
-        for t in range(8):
+        for t in range(16):
             for k in range(corners):
-                e = i * 8 + t
+                e = i * 16 + t
                 picked[k, pl.ds(2 * e, 2), :] = table[pl.ds(conn_ref[k * elements + e], 2), :]
         return carry
 
-    lax.fori_loop(0, elements // 8, pick_elements, 0)
+    lax.fori_loop(0, elements // 16, pick_elements, 0)
     ones = jnp.ones((8, LANES), jnp.bfloat16)
     from_first = lane >= 96
     block = min(512, elements)
@@ -378,10 +378,13 @@
         total = total + arrived[z]
     root = math.sqrt(cases * groups)
     scaling = scale_ref[pl.ds(case * share_rows, share_rows), :]
-    thick_ref[...] = -scaling * total[0:share_rows] / root
+    out_ref[0:share_rows, :] = -scaling * total[0:share_rows] / root
     panel_share = PANELS_DEV // groups
     shift = lax.rem(LANES - case * panel_share, LANES)
-    wash_ref[...] = pltpu.roll(total, shift, 1)[share_rows : share_rows + 1] / root
+    out_ref[share_rows : share_rows + 1, :] = (
+        pltpu.roll(total, shift, 1)[share_rows : share_rows + 1] / root
+    )
+    out_ref[share_rows + 1 : 8, :] = jnp.zeros((7 - share_rows, LANES), jnp.float32)
 
     @pl.when(dom > 0)
     def _():
@@ -424,14 +427,11 @@
     f32 = jnp.float32
     vmem = pl.BlockSpec(memory_space=pltpu.VMEM)
     hbm = pl.BlockSpec(memory_space=pltpu.HBM)
-    thick, panel = pl.pallas_call(
+    out = pl.pallas_call(
         functools.partial(kernel, n_dom, groups),
-        out_shape=(
-            jax.ShapeDtypeStruct((share_rows, LANES), f32),
-            jax.ShapeDtypeStruct((1, LANES), f32),
-        ),
+        out_shape=jax.ShapeDtypeStruct((8, LANES), f32),
         in_specs=[hbm] * 11,
-        out_specs=(vmem, vmem),
+        out_specs=vmem,
         scratch_shapes=[
             pltpu.VMEM((dof * cases, nodes), f32),
             pltpu.VMEM((dof * cases, nodes), f32),
@@ -486,7 +486,10 @@
         spline_count,
         case_weight,
     )
-    return thick.reshape(share_rows * LANES), panel[0, : PANELS_DEV // groups]
+    return (
+        out[:share_rows].reshape(share_rows * LANES),
+        out[share_rows, : PANELS_DEV // groups],
+    )
 
 
 def solution(mesh):

time: 32.2 us -> 32 us (level)
    reshape x0 -> x1, local copies, waits for them, and re-layouts: none -> 1.24 us  [on_device(): out[:share_rows].reshape(share_rows * LANES)]
    unnamed x1 -> x0, local copies, waits for them, and re-layouts: 1.22 us -> none
where the time goes in v4:
time: 32 us; the launch traced here: 31.7 us
  Pallas kernels  28.7 us (90%)
  local copies, waits for them, and re-layouts  2.44 us (8%)
  between operations  0.64 us (2%)
    pallas_call x1, Pallas kernels, on_device(): pl.pallas_call(functools.partial(kernel, n_dom, groups), out_shape=jax.Sh...  28.7 us
    reshape x1, local copies, waits for them, and re-layouts, on_device(): out[:share_rows].reshape(share_rows * LANES)  1.24 us
    squeeze x1, local copies, waits for them, and re-layouts, on_device(): out[share_rows, :PANELS_DEV // groups]  1.2 us

profile of v4, /device:TPU:1, one launch (start us, length us, event | category | flops | bytes accessed | tf_op | source)
XLA Modules:
  0.0 31.7 jit_solution(562375561091800407)
XLA Ops:
  0.6 28.7 %shard_map.122 = f32[8,128]{1,0:T(8,128)} custom-call(f32[96,4096]{1,0:T(8,128)} %bitcast.11, f32[96,4096]{1,0:T(8,128)} %bitcast.12, f32[24,24]{1,0:T(8,128)} %refs_0_.1, f32[8,128]{1,0:T(8,128)} %bitcast.13, s32[8,128]{1,0:T(8,128)} %refs_2_.1, f32[8,128]{1,0:T(8,128)} %refs_3_.1, s32[4,1024]{1,0:T(4,128)} %refs_4_.1, s32[2,512]{1,0:T(2,128)} %refs_5_.1, ...), custom_call_target="tpu_custom_call" | custom-call | tf_op jit(solution)/shard_map/pallas_call | solution.py:430
  29.3 1.2 %slice_bitcast_fusion.1 = f32[16]{0:T(128)} fusion(f32[8,128]{1,0:T(8,128)} %shard_map.122), kind=kLoop, calls=%fused_computation.1 | loop fusion | bytes 128 | tf_op jit(solution)/shard_map/squeeze | solution.py:491
  30.5 1.2 %slice_bitcast_fusion = f32[256]{0:T(256)} fusion(f32[8,128]{1,0:T(8,128)} %shard_map.122), kind=kLoop, calls=%fused_computation | loop fusion | bytes 2048 | tf_op jit(solution)/shard_map/reshape | solution.py:490
